TPU v7x, 512 devices: a whole 4x4x16 slice. The times are simulated.
512 devices in a mesh: row: 16 (over x, y), col: 32 (over z, core).
Axes of the slice: x: 4, y: 4, z: 16, core: 2. Of those that a mesh axis runs over, the one named last changes fastest.
Arguments:
- species: float32 [512, 256, 2048], P(None, 'col', 'row'), may hold values from -26 to 26, as said below
- start_basis: float32 [512, 256], replicated, may hold values from -6 to 6
Outputs:
- core_fibers: float32 [256, 256, 2048], P('row', 'col')
- basis: float32 [512, 256], replicated
Inputs may be any that keep to these rules, and one draw needn't show every extreme that they name: `species`: entries of the slab.
All inputs are finite; a program needn't handle non-finite values.
Results may differ from a plain program's by a relative error of at most 0.00019.
Values sent between devices are 32-bit elements; how exact they have to be, the bound alone decides.
No kernel may reach another device: no remote copies, remote signals or barrier semaphores. Data moves between devices by JAX's collectives and lax.ppermute only.
A program may use at most 64 MiB of HBM per device.

v0:
```python
import jax
import jax.numpy as jnp
from jax import lax
from jax.sharding import PartitionSpec as P

ITERS = 2


def orthonormalize(applied):
    inner_gram = jnp.dot(
        applied.T, applied, precision=lax.Precision.HIGHEST, preferred_element_type=jnp.float32
    )
    small_lower = jnp.linalg.cholesky(inner_gram)
    return jax.scipy.linalg.solve_triangular(small_lower, applied.T, lower=True).T


def power_steps(tri_lower, start_basis):
    current = start_basis
    for sweep_number in range(ITERS):
        halfway = jnp.dot(
            tri_lower.T,
            current,
            precision=lax.Precision.HIGHEST,
            preferred_element_type=jnp.float32,
        )
        applied = jnp.dot(
            tri_lower, halfway, precision=lax.Precision.HIGHEST, preferred_element_type=jnp.float32
        )
        current = orthonormalize(applied)
    return current


def shards(species, start_basis):
    width_x, cells_z, cells_y = species.shape
    fibers = species.reshape(width_x, cells_z * cells_y)
    local_gram = jnp.dot(
        fibers, fibers.T, precision=lax.Precision.HIGHEST, preferred_element_type=jnp.float32
    )
    gram_sum = lax.psum(local_gram, ("row", "col"))
    basis = power_steps(jnp.linalg.cholesky(gram_sum), start_basis)
    core_flat = jnp.dot(
        basis.T, fibers, precision=lax.Precision.HIGHEST, preferred_element_type=jnp.float32
    )
    core_block = core_flat.reshape(basis.shape[1], cells_z, cells_y)
    core_fibers = lax.all_to_all(core_block, "row", split_axis=0, concat_axis=2, tiled=True)
    return (core_fibers, basis)


def solution(mesh):
    in_specs = (P(None, "col", "row"), P())
    out_specs = (P("row", "col", None), P())
    return jax.shard_map(shards, mesh=mesh, in_specs=in_specs, out_specs=out_specs, check_vma=False)
```

profile of v0, /device:TPU:1, one launch (start us, length us, event | category | flops | bytes accessed | tf_op | source)
XLA Modules:
  0.0 744.2 jit_solution(14799633142379794219)
XLA Ops:
  7.2 7.1 fusion.2
  14.4 2.1 copy.41
  16.4 2.3 copy.25
  18.8 468.0 %all-reduce.4.cloned.1.call-done = f32[512,512]{0,1:T(8,128)} async-done(((f32[512,512]{0,1:T(8,128)}), f32[512,512]{0,1:T(8,128)}) %all-reduce.4.cloned.1.call-update) | async-done | bytes 1048592 | tf_op jit(solution)/shard_map/psum | solution.py:39
  486.8 1.6 copy.19
  488.7 1.0 copy-done.2
  489.7 11.7 %cholesky.136 = f32[128,128]{1,0:T(8,128)S(1)} custom-call(f32[128,128]{1,0:T(8,128)S(1)} %cholesky.407), custom_call_target="Cholesky" | custom-call | tf_op jit(solution)/shard_map/jit(cholesky)/cholesky | solution.py:40
  501.4 9.8 %custom-call.32 = f32[1,128,128]{1,2,0:T(8,128)S(1)} custom-call(f32[1,128,128]{2,1,0:T(8,128)S(1)} %get-tuple-element.62), custom_call_target="InvertDiagBlocksLowerTriangular" | custom-call | tf_op jit(solution)/shard_map/jit(cholesky)/cholesky | solution.py:40
  511.3 1.2 constant_dynamic-update-slice_fusion.5
  512.6 1.3 convolution_subtract_fusion.2
  513.9 11.7 %cholesky.159 = f32[128,128]{1,0:T(8,128)S(1)} custom-call(f32[128,128]{1,0:T(8,128)S(1)} %cholesky.411), custom_call_target="Cholesky" | custom-call | tf_op jit(solution)/shard_map/jit(cholesky)/cholesky | solution.py:40
  525.6 10.0 %custom-call.33 = f32[1,128,128]{1,2,0:T(8,128)S(1)} custom-call(f32[1,128,128]{2,1,0:T(8,128)S(1)} %get-tuple-element.59), custom_call_target="InvertDiagBlocksLowerTriangular" | custom-call | tf_op jit(solution)/shard_map/jit(cholesky)/cholesky | solution.py:40
  535.8 1.3 convolution_subtract_fusion.3
  537.1 11.7 %cholesky.294 = f32[128,128]{1,0:T(8,128)S(1)} custom-call(f32[128,128]{1,0:T(8,128)S(1)} %cholesky.416), custom_call_target="Cholesky" | custom-call | tf_op jit(solution)/shard_map/jit(cholesky)/cholesky | solution.py:40
  548.9 0.7 compare_reduce_fusion.5
  549.5 9.8 %custom-call.39 = f32[1,128,128]{1,2,0:T(8,128)S(1)} custom-call(f32[1,128,128]{2,1,0:T(8,128)S(1)} %get-tuple-element.56), custom_call_target="InvertDiagBlocksLowerTriangular" | custom-call | tf_op jit(solution)/shard_map/jit(cholesky)/cholesky/custom-call.9 | solution.py:40
  559.6 1.2 convolution_subtract_fusion.6
  560.8 11.7 %cholesky.307 = f32[128,128]{1,0:T(8,128)S(1)} custom-call(f32[128,128]{1,0:T(8,128)S(1)} %convolution_subtract_fusion.6), custom_call_target="Cholesky" | custom-call | tf_op jit(solution)/shard_map/jit(cholesky)/cholesky | solution.py:40
  572.6 0.7 compare_reduce_fusion.4
  576.4 1.6 fusion.15
  578.0 1.0 fusion.14
  579.0 1.0 fusion.66
  580.2 11.7 %cholesky.357 = f32[128,128]{1,0:T(8,128)S(1)} custom-call(f32[128,128]{1,0:T(8,128)S(1)} %cholesky.420), custom_call_target="Cholesky" | custom-call | tf_op jit(solution)/shard_map/jit(cholesky)/cholesky | solution.py:13
  592.0 0.6 compare_reduce_fusion.3
  592.6 9.8 %custom-call.40 = f32[1,128,128]{1,2,0:T(8,128)S(1)} custom-call(f32[1,128,128]{2,1,0:T(8,128)S(1)} %get-tuple-element.52), custom_call_target="InvertDiagBlocksLowerTriangular" | custom-call | tf_op jit(solution)/shard_map/jit(cholesky)/cholesky/custom-call.9 | solution.py:13
  603.0 11.8 %cholesky.367 = f32[128,128]{1,0:T(8,128)S(1)} custom-call(f32[128,128]{1,0:T(8,128)S(1)} %convolution_subtract_fusion.5), custom_call_target="Cholesky" | custom-call | tf_op jit(solution)/shard_map/jit(cholesky)/cholesky | solution.py:13
  614.8 0.6 compare_reduce_fusion.2
  616.9 4.0 while.4
  617.5 1.4 bitcast_dynamic-update-slice_fusion.4
  619.5 1.4 bitcast_dynamic-update-slice_fusion.4
  620.9 19.7 %custom-call.41 = f32[2,128,128]{1,2,0:T(8,128)S(1)} custom-call(f32[2,128,128]{2,1,0:T(8,128)S(1)} %get-tuple-element.19), custom_call_target="InvertDiagBlocksLowerTriangular" | custom-call | tf_op jit(solution)/shard_map/jit(_solve_triangular)/triangular_solve | solution.py:14
  642.0 1.2 fusion.7
  643.3 1.0 fusion.13
  644.3 1.0 fusion.67
  645.5 11.7 %cholesky.384 = f32[128,128]{1,0:T(8,128)S(1)} custom-call(f32[128,128]{1,0:T(8,128)S(1)} %cholesky.423), custom_call_target="Cholesky" | custom-call | tf_op jit(solution)/shard_map/jit(cholesky)/cholesky | solution.py:13
  657.9 9.8 %custom-call.42 = f32[1,128,128]{1,2,0:T(8,128)S(1)} custom-call(f32[1,128,128]{2,1,0:T(8,128)S(1)} %get-tuple-element.48), custom_call_target="InvertDiagBlocksLowerTriangular" | custom-call | tf_op jit(solution)/shard_map/jit(cholesky)/cholesky/custom-call.9 | solution.py:13
  668.2 11.9 %cholesky.394 = f32[128,128]{1,0:T(8,128)S(1)} custom-call(f32[128,128]{1,0:T(8,128)S(1)} %convolution_subtract_fusion.4), custom_call_target="Cholesky" | custom-call | tf_op jit(solution)/shard_map/jit(cholesky)/cholesky | solution.py:13
  680.1 0.6 compare_reduce_fusion
  682.1 4.0 while.5
  682.7 1.4 bitcast_dynamic-update-slice_fusion.5
  684.7 1.4 bitcast_dynamic-update-slice_fusion.5
  686.1 19.7 %custom-call.43 = f32[2,128,128]{1,2,0:T(8,128)S(1)} custom-call(f32[2,128,128]{2,1,0:T(8,128)S(1)} %get-tuple-element.20), custom_call_target="InvertDiagBlocksLowerTriangular" | custom-call | tf_op jit(solution)/shard_map/jit(_solve_triangular)/triangular_solve | solution.py:14
  707.3 3.5 fusion.11
  710.8 1.6 copy.26
  712.4 6.2 all-to-all-start
  718.6 1.0 copy.28
  719.6 16.4 %all-to-all-done = f32[256,8,128]{2,1,0:T(8,128)S(1)} async-done(((f32[256,8,128]{2,1,0:T(8,128)}), f32[256,8,128]{2,1,0:T(8,128)S(1)}, u32[]{:S(2)}, u32[]{:S(2)}) %all-to-all-start) | async-done | bytes 1048608 | tf_op jit(solution)/shard_map/all_to_all | solution.py:45
  736.1 1.1 copy.42
  (57 shorter events, 9.2 us)
Async XLA Ops:
  7.2 569.2 %copy-start = (f32[512,256]{1,0:T(8,128)S(1)}, f32[512,256]{1,0:T(8,128)}, u32[]{:S(2)}) copy-start(f32[512,256]{1,0:T(8,128)} %param.8) | copy-start | bytes 1572868
  7.2 479.6 %all-reduce.4.cloned.1.call-start = ((), (), s32[]{:S(2)}) async-start(), calls=%async_computation.1 | async-start | bytes 2097152 | tf_op jit(solution)/shard_map/psum | solution.py:39
  486.8 1.7 copy-start.1
  488.7 1.0 copy-start.2
  712.4 23.7 %all-to-all-start = ((f32[256,8,128]{2,1,0:T(8,128)}), f32[256,8,128]{2,1,0:T(8,128)S(1)}, u32[]{:S(2)}, u32[]{:S(2)}) async-start(f32[256,8,128]{2,1,0:T(8,128)} %copy.26), calls=%async_computation | async-start | bytes 2097152 | tf_op jit(solution)/shard_map/all_to_all | solution.py:45
Sparse Core Ops, SparseCore 0:
  14.5 472.2 all-reduce.3
where the time goes:
time: 749 us; the launch traced here: 744 us
  waiting for transfers between devices  484 us (65%)
  other arithmetic  188 us (25%)
  matrix products  26.7 us (4%)
  between operations  19.8 us (3%)
  local copies, waits for them, and re-layouts  19.1 us (3%)
    psum x1, waiting for transfers between devices, shards(): gram_sum = lax.psum(local_gram, ('row', 'col'))  468 us
    another operation x14, other arithmetic, shards(): basis = power_steps(jnp.linalg.cholesky(gram_sum), start_basis)  78.5 us
    another operation x14, other arithmetic, orthonormalize(): small_lower = jnp.linalg.cholesky(inner_gram)  69.5 us
    another operation x5, other arithmetic, orthonormalize(): jax.scipy.linalg.solve_triangular(small_lower, applied.T, lower=True)  39.4 us
    all_to_all x1, waiting for transfers between devices, shards(): lax.all_to_all(core_block, 'row', split_axis=0, concat_axis=2, tiled=True)  16.4 us
  transfers between devices with their start and end apart: 2, of which 2 were waited for; matrix products, arithmetic and copies ran while one was open for 1% of the time, Pallas kernels for 0%

commit v1 on v0

--- a/solution.py
+++ b/solution.py
@@ -36,7 +36,7 @@
     local_gram = jnp.dot(
         fibers, fibers.T, precision=lax.Precision.HIGHEST, preferred_element_type=jnp.float32
     )
-    gram_sum = lax.psum(local_gram, ("row", "col"))
+    gram_sum = lax.psum(lax.psum(local_gram, "col"), "row")
     basis = power_steps(jnp.linalg.cholesky(gram_sum), start_basis)
     core_flat = jnp.dot(
         basis.T, fibers, precision=lax.Precision.HIGHEST, preferred_element_type=jnp.float32

time: 749 us -> 609 us (0.81)
  waiting for transfers between devices: 484 us -> 345 us
    psum x1 -> x2, waiting for transfers between devices: 468 us -> 331 us  [shards(): gram_sum = lax.psum(lax.psum(local_gram, 'col'), 'row')]
  transfers between devices with their start and end apart: 2 -> 3, of which waited for: 2 -> 3; matrix products, arithmetic and copies ran while one was open for 1% -> 1% of each run, Pallas kernels for 0% -> 0%
where the time goes in v1:
time: 609 us; the launch traced here: 603 us
  waiting for transfers between devices  345 us (57%)
  other arithmetic  188 us (31%)
  matrix products  26.7 us (4%)
  between operations  19.8 us (3%)
  local copies, waits for them, and re-layouts  19.1 us (3%)
    psum x2, waiting for transfers between devices, shards(): gram_sum = lax.psum(lax.psum(local_gram, 'col'), 'row')  331 us
    another operation x14, other arithmetic, shards(): basis = power_steps(jnp.linalg.cholesky(gram_sum), start_basis)  78.5 us
    another operation x14, other arithmetic, orthonormalize(): small_lower = jnp.linalg.cholesky(inner_gram)  69.5 us
    another operation x5, other arithmetic, orthonormalize(): jax.scipy.linalg.solve_triangular(small_lower, applied.T, lower=True)  39.4 us
    all_to_all x1, waiting for transfers between devices, shards(): lax.all_to_all(core_block, 'row', split_axis=0, concat_axis=2, tiled=True)  13.5 us
  transfers between devices with their start and end apart: 3, of which 3 were waited for; matrix products, arithmetic and copies ran while one was open for 1% of the time, Pallas kernels for 0%

profile of v1, /device:TPU:1, one launch (start us, length us, event | category | flops | bytes accessed | tf_op | source)
XLA Modules:
  0.0 602.7 jit_solution(16979963395513595109)
XLA Ops:
  7.2 7.1 %fusion.2 = f32[512,512]{0,1:T(8,128)} fusion(f32[512,8,128]{2,1,0:T(8,128)} %param.7), kind=kOutput, calls=%fused_computation.7 | convolution fusion | flops 3221225472 | bytes 3145728 | tf_op jit(solution)/shard_map/dot_general | solution.py:36
  14.4 215.9 %all-reduce.5.cloned.1.call-done = f32[512,512]{0,1:T(8,128)} async-done(((f32[512,512]{0,1:T(8,128)}), f32[512,512]{0,1:T(8,128)}) %all-reduce.5.cloned.1.call-update) | async-done | bytes 1048592 | tf_op jit(solution)/shard_map/psum | solution.py:39
  230.4 2.1 copy.41
  232.4 2.3 copy.25
  234.8 115.3 %all-reduce.7.cloned.1.call-done = f32[512,512]{0,1:T(8,128)} async-done(((f32[512,512]{0,1:T(8,128)}), f32[512,512]{0,1:T(8,128)}) %all-reduce.7.cloned.1.call-update) | async-done | bytes 1048592 | tf_op jit(solution)/shard_map/psum | solution.py:39
  350.0 1.6 copy.19
  351.9 1.0 copy-done.2
  352.9 11.7 %cholesky.136 = f32[128,128]{1,0:T(8,128)S(1)} custom-call(f32[128,128]{1,0:T(8,128)S(1)} %cholesky.407), custom_call_target="Cholesky" | custom-call | tf_op jit(solution)/shard_map/jit(cholesky)/cholesky | solution.py:40
  364.6 9.8 %custom-call.32 = f32[1,128,128]{1,2,0:T(8,128)S(1)} custom-call(f32[1,128,128]{2,1,0:T(8,128)S(1)} %get-tuple-element.62), custom_call_target="InvertDiagBlocksLowerTriangular" | custom-call | tf_op jit(solution)/shard_map/jit(cholesky)/cholesky | solution.py:40
  374.6 1.2 constant_dynamic-update-slice_fusion.5
  375.8 1.3 convolution_subtract_fusion.2
  377.1 11.7 %cholesky.159 = f32[128,128]{1,0:T(8,128)S(1)} custom-call(f32[128,128]{1,0:T(8,128)S(1)} %cholesky.411), custom_call_target="Cholesky" | custom-call | tf_op jit(solution)/shard_map/jit(cholesky)/cholesky | solution.py:40
  388.8 10.0 %custom-call.33 = f32[1,128,128]{1,2,0:T(8,128)S(1)} custom-call(f32[1,128,128]{2,1,0:T(8,128)S(1)} %get-tuple-element.59), custom_call_target="InvertDiagBlocksLowerTriangular" | custom-call | tf_op jit(solution)/shard_map/jit(cholesky)/cholesky | solution.py:40
  399.1 1.3 convolution_subtract_fusion.3
  400.4 11.7 %cholesky.294 = f32[128,128]{1,0:T(8,128)S(1)} custom-call(f32[128,128]{1,0:T(8,128)S(1)} %cholesky.416), custom_call_target="Cholesky" | custom-call | tf_op jit(solution)/shard_map/jit(cholesky)/cholesky | solution.py:40
  412.1 0.7 compare_reduce_fusion.5
  412.8 9.8 %custom-call.39 = f32[1,128,128]{1,2,0:T(8,128)S(1)} custom-call(f32[1,128,128]{2,1,0:T(8,128)S(1)} %get-tuple-element.56), custom_call_target="InvertDiagBlocksLowerTriangular" | custom-call | tf_op jit(solution)/shard_map/jit(cholesky)/cholesky/custom-call.9 | solution.py:40
  422.8 1.2 convolution_subtract_fusion.6
  424.0 11.7 %cholesky.307 = f32[128,128]{1,0:T(8,128)S(1)} custom-call(f32[128,128]{1,0:T(8,128)S(1)} %convolution_subtract_fusion.6), custom_call_target="Cholesky" | custom-call | tf_op jit(solution)/shard_map/jit(cholesky)/cholesky | solution.py:40
  435.8 0.7 compare_reduce_fusion.4
  439.6 1.6 fusion.15
  441.3 1.0 fusion.14
  442.3 1.0 fusion.66
  443.5 11.7 %cholesky.357 = f32[128,128]{1,0:T(8,128)S(1)} custom-call(f32[128,128]{1,0:T(8,128)S(1)} %cholesky.420), custom_call_target="Cholesky" | custom-call | tf_op jit(solution)/shard_map/jit(cholesky)/cholesky | solution.py:13
  455.2 0.6 compare_reduce_fusion.3
  455.9 9.8 %custom-call.40 = f32[1,128,128]{1,2,0:T(8,128)S(1)} custom-call(f32[1,128,128]{2,1,0:T(8,128)S(1)} %get-tuple-element.52), custom_call_target="InvertDiagBlocksLowerTriangular" | custom-call | tf_op jit(solution)/shard_map/jit(cholesky)/cholesky/custom-call.9 | solution.py:13
  466.2 11.8 %cholesky.367 = f32[128,128]{1,0:T(8,128)S(1)} custom-call(f32[128,128]{1,0:T(8,128)S(1)} %convolution_subtract_fusion.5), custom_call_target="Cholesky" | custom-call | tf_op jit(solution)/shard_map/jit(cholesky)/cholesky | solution.py:13
  478.1 0.6 compare_reduce_fusion.2
  480.1 4.0 while.4
  480.7 1.4 bitcast_dynamic-update-slice_fusion.4
  482.7 1.4 bitcast_dynamic-update-slice_fusion.4
  484.1 19.7 %custom-call.41 = f32[2,128,128]{1,2,0:T(8,128)S(1)} custom-call(f32[2,128,128]{2,1,0:T(8,128)S(1)} %get-tuple-element.19), custom_call_target="InvertDiagBlocksLowerTriangular" | custom-call | tf_op jit(solution)/shard_map/jit(_solve_triangular)/triangular_solve | solution.py:14
  505.3 1.2 fusion.7
  506.5 1.0 fusion.13
  507.5 1.0 fusion.67
  508.7 11.7 %cholesky.384 = f32[128,128]{1,0:T(8,128)S(1)} custom-call(f32[128,128]{1,0:T(8,128)S(1)} %cholesky.423), custom_call_target="Cholesky" | custom-call | tf_op jit(solution)/shard_map/jit(cholesky)/cholesky | solution.py:13
  521.1 9.8 %custom-call.42 = f32[1,128,128]{1,2,0:T(8,128)S(1)} custom-call(f32[1,128,128]{2,1,0:T(8,128)S(1)} %get-tuple-element.48), custom_call_target="InvertDiagBlocksLowerTriangular" | custom-call | tf_op jit(solution)/shard_map/jit(cholesky)/cholesky/custom-call.9 | solution.py:13
  531.4 11.9 %cholesky.394 = f32[128,128]{1,0:T(8,128)S(1)} custom-call(f32[128,128]{1,0:T(8,128)S(1)} %convolution_subtract_fusion.4), custom_call_target="Cholesky" | custom-call | tf_op jit(solution)/shard_map/jit(cholesky)/cholesky | solution.py:13
  545.4 4.0 while.5
  546.0 1.4 bitcast_dynamic-update-slice_fusion.5
  548.0 1.4 bitcast_dynamic-update-slice_fusion.5
  549.4 19.7 %custom-call.43 = f32[2,128,128]{1,2,0:T(8,128)S(1)} custom-call(f32[2,128,128]{2,1,0:T(8,128)S(1)} %get-tuple-element.20), custom_call_target="InvertDiagBlocksLowerTriangular" | custom-call | tf_op jit(solution)/shard_map/jit(_solve_triangular)/triangular_solve | solution.py:14
  570.5 3.5 fusion.11
  574.0 1.6 copy.26
  575.6 4.3 all-to-all-start
  580.0 1.0 copy.28
  581.0 13.5 %all-to-all-done = f32[256,8,128]{2,1,0:T(8,128)S(1)} async-done(((f32[256,8,128]{2,1,0:T(8,128)}), f32[256,8,128]{2,1,0:T(8,128)S(1)}, u32[]{:S(2)}, u32[]{:S(2)}) %all-to-all-start) | async-done | bytes 1048608 | tf_op jit(solution)/shard_map/all_to_all | solution.py:45
  594.5 1.1 copy.42
  (60 shorter events, 9.9 us)
Async XLA Ops:
  7.2 432.5 %copy-start = (f32[512,256]{1,0:T(8,128)S(1)}, f32[512,256]{1,0:T(8,128)}, u32[]{:S(2)}) copy-start(f32[512,256]{1,0:T(8,128)} %param.8) | copy-start | bytes 1572868
  7.2 223.2 %all-reduce.5.cloned.1.call-start = ((), (), s32[]{:S(2)}) async-start(), calls=%async_computation.1 | async-start | bytes 2097152 | tf_op jit(solution)/shard_map/psum | solution.py:39
  14.4 335.6 %all-reduce.7.cloned.1.call-start = ((), (), s32[]{:S(2)}) async-start(), calls=%async_computation.2 | async-start | bytes 2097152 | tf_op jit(solution)/shard_map/psum | solution.py:39
  350.0 1.7 copy-start.1
  351.9 1.0 copy-start.2
  575.6 18.9 %all-to-all-start = ((f32[256,8,128]{2,1,0:T(8,128)}), f32[256,8,128]{2,1,0:T(8,128)S(1)}, u32[]{:S(2)}, u32[]{:S(2)}) async-start(f32[256,8,128]{2,1,0:T(8,128)} %copy.26), calls=%async_computation | async-start | bytes 2097152 | tf_op jit(solution)/shard_map/all_to_all | solution.py:45
Sparse Core Ops, SparseCore 0:
  14.5 215.8 all-reduce.4
  233.9 116.0 all-reduce.6
